TPU v7x, 32 devices: a whole 2x2x4 slice. The times are simulated.
32 devices in a mesh: groups: 2 (over x), slab: 8 (over z, y), cross: 2 (over core).
Axes of the slice: x: 2, y: 2, z: 4, core: 2. Of those that a mesh axis runs over, the one named last changes fastest.
Arguments:
- mode_shapes: float32 [32, 3, 4096], P(None, None, ('slab', 'cross')), may hold values from -16 to 16, as said below
- stencil: int32 [3, 8192], P(None, ('slab', 'cross')), may hold values from 0 to 255
- stencil_weight: float32 [3, 8192], P(None, ('slab', 'cross')), may hold values from 0.2 to 1
- owner_slab: int32 [8192, 1], P(('slab', 'cross')), may hold values from 0 to 7; in each aligned block of 512 rows (0 to 511, 512 to 1023, ...) at most 128 rows name the same one
- target_cell: int32 [8192], P(('slab', 'cross')), may hold values from 0 to 4095
- neighbour_codes: int32 [7, 256, 256], P(None, 'slab', 'cross'), may hold values from 0 to 9, as said below
- jacobian: bfloat16 [14, 5, 5, 256, 256], P('groups', None, None, 'slab', 'cross'), parts along dimension 0, may hold values from -1.25 to 1.25
- lift_matrix: bfloat16 [10, 3, 256, 256], P('groups', None, 'slab', 'cross'), parts along dimension 0, may hold values from -3.5 to 3.5
- pod_basis: bfloat16 [10, 256, 256, 128], P('groups', 'slab', 'cross'), parts along dimension 0, may hold values from -0.03125 to 0.03125
Outputs:
- induced: float32 [64, 5, 256, 256], P('groups', None, 'slab', 'cross'), parts along dimension 0
- reduced: float32 [64, 128], P('groups'), parts along dimension 0
There are 2 independent parts, one for each index of `groups`. A program takes and returns all parts, laid end to end along the dimension named above; an argument that names none is the same for every part. Nothing has to cross between parts.
Inputs may be any that keep to these rules, and one draw needn't show every extreme that they name: `mode_shapes`: mode shapes whose magnitude varies over the nodes. `stencil`: entries name structural nodes of the same device's block of 256 nodes. `owner_slab`: in each aligned block of 512 rows (the rows of one device) no slab is named by more than 128 rows. `target_cell`: the owning device is the one of slab owner_slab with the surface node's own cross index. `neighbour_codes`: slot 0 holds code 4 (the cell itself); the live codes of a cell are distinct and come first, 4 or more of them; 9 marks an unused slot.
All inputs are finite; a program needn't handle non-finite values.
Results may differ from a plain program's by a relative error of at most 0.0003.
Values may be sent and summed in bfloat16 or wider, within the bound.
A program may use at most 128 MiB of HBM per device.

v0:
```python
import functools

import jax
import jax.numpy as jnp
from jax import lax
from jax.experimental import pallas as pl
from jax.experimental.pallas import tpu as pltpu
from jax.sharding import PartitionSpec as P

SWEEPS = 4


SPREAD = 0.24

RIM = SWEEPS + 1

LANES = 128

MESH = pl.DeviceIdType.MESH

NT = (((1,), (1,)), ((), ()))


def split_2(value):
    high = value.astype(jnp.bfloat16)
    low = (value - high.astype(jnp.float32)).astype(jnp.bfloat16)
    return high, low


def route_kernel(
    slabs,
    rows,
    modes_dim,
    comps,
    node_total,
    modes_ref,
    stencil_ref,
    weight_ref,
    owner_ref,
    target_ref,
    lift_ref,
    field_ref,
    scale_ref,
    send_buf,
    recv_buf,
    arrived,
    labels,
    squares,
    send_sem,
    recv_sem,
    edge_send,
    edge_recv,
    pair_send,
    pair_recv,
    sq_send,
    sq_recv,
):
    me = lax.axis_index("slab")
    mine = lax.axis_index("cross")
    other = 1 - mine
    nodes = modes_ref.shape[1]
    surf = stencil_ref.shape[1]
    data = modes_dim * comps

    barrier = pltpu.get_barrier_semaphore()
    for k in range(1, slabs):
        pl.semaphore_signal(
            barrier, inc=1, device_id={"slab": lax.rem(me + k, slabs)}, device_id_type=MESH
        )
    pl.semaphore_signal(barrier, inc=1, device_id={"cross": other}, device_id_type=MESH)

    node_id = lax.broadcasted_iota(jnp.int32, (nodes, surf), 0)
    mix = jnp.zeros((nodes, surf), jnp.float32)
    for j in range(stencil_ref.shape[0]):
        mix = mix + jnp.where(stencil_ref[j : j + 1, :] == node_id, weight_ref[j : j + 1, :], 0.0)
    surface = jnp.dot(
        modes_ref[...], mix, precision=lax.Precision.HIGHEST, preferred_element_type=jnp.float32
    )
    owner = owner_ref[...]
    slab_id = lax.broadcasted_iota(jnp.int32, (slabs, surf), 0)
    named = (owner == slab_id).astype(jnp.float32)
    before = (
        lax.broadcasted_iota(jnp.int32, (surf, surf), 0)
        < lax.broadcasted_iota(jnp.int32, (surf, surf), 1)
    ).astype(jnp.bfloat16)
    ahead = jnp.dot(named.astype(jnp.bfloat16), before, preferred_element_type=jnp.float32)
    rank = jnp.sum(ahead * named, axis=0, keepdims=True).astype(jnp.int32)
    position = owner * LANES + rank
    target = target_ref[...]
    target_low = lax.rem(target, 64)
    row_id = lax.broadcasted_iota(jnp.int32, surface.shape, 0)
    high = surface.astype(jnp.bfloat16).astype(jnp.float32)
    low = surface - high
    high = jnp.where(row_id == data, (target - target_low).astype(jnp.float32), high)
    high = jnp.where(row_id == data + 1, 1.0, high)
    low = jnp.where(row_id == data, target_low.astype(jnp.float32), low)
    both = jnp.concatenate([high, low], axis=0).astype(jnp.bfloat16)
    modes = modes_ref[...]
    square_row = lax.dot_general(
        jnp.ones((8, nodes), jnp.float32),
        modes * modes,
        NT,
        precision=lax.Precision.HIGHEST,
        preferred_element_type=jnp.float32,
    )[0:1]
    slot_id = lax.broadcasted_iota(jnp.int32, (LANES, surf), 0)
    out_rows = send_buf.shape[1]
    out_id = lax.broadcasted_iota(jnp.int32, (out_rows, LANES), 0)

    pl.semaphore_wait(barrier, slabs)
    copies = []
    for step in range(slabs):
        k = (step + 1) % slabs
        dest = lax.rem(me + k, slabs)
        onehot = (position == slot_id + dest * LANES).astype(jnp.float32).astype(jnp.bfloat16)
        packed = lax.dot_general(both, onehot, NT, preferred_element_type=jnp.float32)
        block = packed[0:out_rows] + packed[LANES : LANES + out_rows]
        empty = 1.0 - block[data + 1 : data + 2]
        block = jnp.where(out_id == data, block - 65536.0 * empty, block)
        block = jnp.where(out_id == data + 2, square_row, block)
        if k == 0:
            recv_buf[0] = block
        else:
            send_buf[k] = block
            copy = pltpu.make_async_remote_copy(
                src_ref=send_buf.at[k],
                dst_ref=recv_buf.at[k],
                send_sem=send_sem.at[k],
                recv_sem=recv_sem.at[k],
                device_id={"slab": dest},
                device_id_type=MESH,
            )
            copy.start()
            copies.append(copy)

    field_ref[mine, RIM : RIM + rows, data:, :] = lift_ref[...]

    @pl.when(me == 0)
    def _():
        field_ref[mine, 0:RIM] = jnp.zeros((RIM,) + field_ref.shape[2:], jnp.float32)

    @pl.when(me == slabs - 1)
    def _():
        field_ref[mine, RIM + rows :] = jnp.zeros((RIM,) + field_ref.shape[2:], jnp.float32)

    total = square_row
    for k in range(slabs):
        if k > 0:
            copies[k - 1].wait_recv()
            total = total + recv_buf[k, data + 2 : data + 3]
        head, tail = split_2(recv_buf[k, 0:data])
        arrived[0:data, k * LANES : (k + 1) * LANES] = head
        arrived[data:, k * LANES : (k + 1) * LANES] = tail
        labels[0:1, k * LANES : (k + 1) * LANES] = recv_buf[k, data : data + 1].astype(jnp.int32)

    squares[0] = jnp.broadcast_to(total, (8, LANES))
    sq_copy = pltpu.make_async_remote_copy(
        src_ref=squares.at[0],
        dst_ref=squares.at[1],
        send_sem=sq_send,
        recv_sem=sq_recv,
        device_id={"cross": other},
        device_id_type=MESH,
    )
    sq_copy.start()

    cell_id = lax.broadcasted_iota(jnp.int32, (2 * LANES, slabs * LANES), 0)
    pairs = rows // 2

    def deposit(i, carry):
        pair = lax.rem(i + pairs - 3, pairs)
        hit = (labels[0:1, :] == cell_id + pair * (2 * LANES)).astype(jnp.float32)
        got = lax.dot_general(
            arrived[...], hit.astype(jnp.bfloat16), NT, preferred_element_type=jnp.float32
        )
        got = got[0:data] + got[data:]
        field_ref[mine, RIM + 2 * pair, 0:data, :] = got[:, 0:LANES]
        field_ref[mine, RIM + 2 * pair + 1, 0:data, :] = got[:, LANES:]
        return carry

    up = pltpu.make_async_remote_copy(
        src_ref=field_ref.at[mine, pl.ds(rows, RIM)],
        dst_ref=field_ref.at[mine, pl.ds(0, RIM)],
        send_sem=edge_send.at[0],
        recv_sem=edge_recv.at[0],
        device_id={"slab": lax.rem(me + 1, slabs)},
        device_id_type=MESH,
    )
    down = pltpu.make_async_remote_copy(
        src_ref=field_ref.at[mine, pl.ds(RIM, RIM)],
        dst_ref=field_ref.at[mine, pl.ds(RIM + rows, RIM)],
        send_sem=edge_send.at[1],
        recv_sem=edge_recv.at[1],
        device_id={"slab": lax.rem(me + slabs - 1, slabs)},
        device_id_type=MESH,
    )

    def across(n, start, size):
        return pltpu.make_async_remote_copy(
            src_ref=field_ref.at[mine, pl.ds(start, size)],
            dst_ref=field_ref.at[mine, pl.ds(start, size)],
            send_sem=pair_send.at[n],
            recv_sem=pair_recv.at[n],
            device_id={"cross": other},
            device_id_type=MESH,
        )

    middle = across(0, RIM, rows)
    low_rim = across(1, 0, RIM)
    high_rim = across(2, RIM + rows, RIM)

    lax.fori_loop(0, 3, deposit, 0)

    @pl.when(me < slabs - 1)
    def _():
        up.start()

    lax.fori_loop(3, 6, deposit, 0)

    @pl.when(me > 0)
    def _():
        down.start()

    lax.fori_loop(6, pairs, deposit, 0)
    middle.start()

    @pl.when(me > 0)
    def _():
        up.wait_recv()

    low_rim.start()

    @pl.when(me < slabs - 1)
    def _():
        down.wait_recv()

    high_rim.start()

    sq_copy.wait()
    whole = squares[0, 0:1] + squares[1, 0:1]
    lane = lax.broadcasted_iota(jnp.int32, (modes_dim, LANES), 1)
    mode = lax.broadcasted_iota(jnp.int32, (modes_dim, LANES), 0)
    per_mode = jnp.sum(
        jnp.where((lax.rem(lane, modes_dim) == mode) & (lane < data), whole, 0.0),
        axis=1,
        keepdims=True,
    )
    inverse = 1.0 / jnp.sqrt(per_mode / node_total + 1e-06)
    scale_ref[...] = jnp.broadcast_to(inverse, scale_ref.shape)

    for copy in copies:
        copy.wait_send()

    @pl.when(me < slabs - 1)
    def _():
        up.wait_send()

    @pl.when(me > 0)
    def _():
        down.wait_send()

    middle.wait()
    low_rim.wait()
    high_rim.wait()


def local_kernel(
    slabs,
    rows,
    modes_dim,
    comps,
    variables,
    field_ref,
    scale_ref,
    codes_ref,
    jac_ref,
    pod_ref,
    induced_ref,
    partial_ref,
    ping,
    pong,
    state,
    blocks,
):
    me = lax.axis_index("slab")
    mine = lax.axis_index("cross")
    other = 1 - mine
    data = modes_dim * comps
    planes = rows + 2 * RIM
    lane = lax.broadcasted_iota(jnp.int32, (modes_dim, LANES), 1)
    first, last = lane == 0, lane == LANES - 1
    square = variables * variables

    def select(pair, carry):
        for x0 in range(0, rows, 8):
            chosen = [jac_ref[k, pair, x0 : x0 + 8, :].astype(jnp.float32) for k in range(7)]
            codes = [codes_ref[k, x0 : x0 + 8, :] for k in range(7)]
            for code in range(9):
                value = jnp.zeros((8, LANES), jnp.float32)
                for k in range(7):
                    value = jnp.where(codes[k] == code, chosen[k], value)
                blocks[code * square + pair, x0 : x0 + 8, :] = value
        return carry

    lax.fori_loop(0, square, select, 0)

    def sweep(source, result, edge):
        def plane(x, carry):
            at = x - RIM + me * rows
            inside = ((at >= 0) & (at < slabs * rows)).astype(jnp.float32)
            for comp in range(comps):
                part = pl.ds(comp * modes_dim, modes_dim)
                left, right = source[0, x, part, :], source[1, x, part, :]
                left_up, right_up = pltpu.roll(left, 1, 1), pltpu.roll(right, 1, 1)
                left_down = pltpu.roll(left, LANES - 1, 1)
                right_down = pltpu.roll(right, LANES - 1, 1)
                near_left = jnp.where(first, 0.0, left_up) + jnp.where(last, right_down, left_down)
                near_right = jnp.where(first, left_up, right_up) + jnp.where(last, 0.0, right_down)
                for tile, near in ((0, near_left), (1, near_right)):
                    near = near + source[tile, x - 1, part, :] + source[tile, x + 1, part, :]
                    result[tile, x, part, :] = (
                        field_ref[tile, x, part, :] + SPREAD * near
                    ) * inside
            return carry

        lax.fori_loop(edge, planes - edge, plane, 0)

    sweep(field_ref, ping, 1)
    sweep(ping, pong, 2)
    sweep(pong, ping, 3)
    sweep(ping, pong, 4)

    here = (mine == 0).astype(jnp.float32)
    there = 1.0 - here

    def lift(x, carry):
        for b in range(variables):
            own = jnp.zeros((modes_dim, LANES), jnp.float32)
            far = jnp.zeros((modes_dim, LANES), jnp.float32)
            for comp in range(comps):
                part = pl.ds(comp * modes_dim, modes_dim)
                row = pl.ds(data + comp * variables + b, 1)
                own = own + field_ref[mine, x + RIM - 1, row, :] * pong[mine, x + RIM - 1, part, :]
                far = (
                    far + field_ref[other, x + RIM - 1, row, :] * pong[other, x + RIM - 1, part, :]
                )
            state[1, x, b] = own
            state[0, x, b] = jnp.where(first, pltpu.roll(far, 1, 1) * there, pltpu.roll(own, 1, 1))
            state[2, x, b] = jnp.where(
                last, pltpu.roll(far, LANES - 1, 1) * here, pltpu.roll(own, LANES - 1, 1)
            )
        return carry

    lax.fori_loop(0, rows + 2, lift, 0)

    stride = variables * rows

    def apply(x, total):
        sums = [jnp.zeros((modes_dim, LANES), jnp.float32) for _ in range(variables)]
        for code in range(9):
            for a in range(variables):
                value = state[code % 3, x + code // 3, a]
                for b in range(variables):
                    gain = blocks[code * square + b * variables + a, pl.ds(x, 1), :]
                    sums[b] = sums[b] + gain * value
        for b in range(variables):
            result = sums[b] * scale_ref[...]
            induced_ref[pl.ds(b * rows + x, modes_dim, stride=stride), :] = result
            high, low = split_2(result)
            total = total + jnp.dot(
                jnp.concatenate([high, low], axis=0),
                pod_ref[b, x],
                preferred_element_type=jnp.float32,
            )
        return total

    total = lax.fori_loop(
        0, rows, apply, jnp.zeros((2 * modes_dim, partial_ref.shape[1]), jnp.float32)
    )
    partial_ref[...] = total[0:modes_dim] + total[modes_dim:]


def sum_kernel(
    slabs, crosses, part_ref, out_ref, got, mine_sum, send_sem, recv_sem, back_send, back_recv
):
    me = lax.axis_index("slab") * crosses + lax.axis_index("cross")
    count = slabs * crosses

    def peer(k):
        at = lax.rem(me + k, count)
        return at, {"slab": lax.div(at, crosses), "cross": lax.rem(at, crosses)}

    barrier = pltpu.get_barrier_semaphore()
    for k in range(1, count):
        pl.semaphore_signal(barrier, inc=1, device_id=peer(k)[1], device_id_type=MESH)
    pl.semaphore_wait(barrier, count - 1)
    copies = []
    for k in range(1, count):
        at, device = peer(k)
        copy = pltpu.make_async_remote_copy(
            src_ref=part_ref.at[at],
            dst_ref=got.at[k],
            send_sem=send_sem.at[k],
            recv_sem=recv_sem.at[k],
            device_id=device,
            device_id_type=MESH,
        )
        copy.start()
        copies.append(copy)
    total = part_ref[me]
    for k in range(1, count):
        copies[k - 1].wait_recv()
        total = total + got[k]
    mine_sum[...] = total
    out_ref[me] = total
    backs = []
    for k in range(1, count):
        at, device = peer(k)
        copy = pltpu.make_async_remote_copy(
            src_ref=mine_sum,
            dst_ref=out_ref.at[me],
            send_sem=back_send.at[k],
            recv_sem=back_recv.at[k],
            device_id=device,
            device_id_type=MESH,
        )
        copy.start()
        backs.append(copy)
    for copy in copies:
        copy.wait_send()
    for copy in backs:
        copy.wait()


VMEM = pl.BlockSpec(memory_space=pltpu.VMEM)


def fast_body(
    mode_shapes,
    stencil,
    stencil_weight,
    owner_slab,
    target_cell,
    neighbour_codes,
    jacobian,
    lift_matrix,
    pod_basis,
):
    slabs = lax.axis_size("slab")
    crosses = lax.axis_size("cross")
    modes_dim, comps, nodes = mode_shapes.shape
    surf = owner_slab.shape[0]
    rows, cols = neighbour_codes.shape[1:]
    variables = lift_matrix.shape[0]
    pod = pod_basis.shape[-1]
    data = modes_dim * comps
    lift_rows = 16
    planes = rows + 2 * RIM
    count = slabs * crosses
    modes = jnp.pad(
        mode_shapes.transpose(1, 0, 2).reshape(data, nodes), ((0, LANES - data), (0, 0))
    )
    lift = jnp.pad(
        lift_matrix.transpose(2, 1, 0, 3).reshape(rows, comps * variables, cols),
        ((0, 0), (0, lift_rows - comps * variables), (0, 0)),
    ).astype(jnp.float32)
    dma = pltpu.SemaphoreType.DMA
    field, scale = pl.pallas_call(
        functools.partial(
            route_kernel, slabs, rows, modes_dim, comps, float(comps * nodes * count)
        ),
        out_shape=(
            jax.ShapeDtypeStruct((crosses, planes, data + lift_rows, cols), jnp.float32),
            jax.ShapeDtypeStruct((modes_dim, LANES), jnp.float32),
        ),
        in_specs=[VMEM] * 6,
        out_specs=(VMEM, VMEM),
        scratch_shapes=[
            pltpu.VMEM((slabs, data + 8, LANES), jnp.float32),
            pltpu.VMEM((slabs, data + 8, LANES), jnp.float32),
            pltpu.VMEM((2 * data, slabs * LANES), jnp.bfloat16),
            pltpu.VMEM((8, slabs * LANES), jnp.int32),
            pltpu.VMEM((2, 8, LANES), jnp.float32),
            dma((slabs,)),
            dma((slabs,)),
            dma((2,)),
            dma((2,)),
            dma((3,)),
            dma((3,)),
            dma,
            dma,
        ],
        compiler_params=pltpu.CompilerParams(
            collective_id=0, has_side_effects=True, vmem_limit_bytes=40 * 1024 * 1024
        ),
    )(
        modes,
        stencil,
        stencil_weight,
        owner_slab.reshape(1, surf),
        target_cell.reshape(1, surf),
        lift,
    )
    scratch = pltpu.VMEM((crosses, planes, data, cols), jnp.float32)
    induced, partial_value = pl.pallas_call(
        functools.partial(local_kernel, slabs, rows, modes_dim, comps, variables),
        out_shape=(
            jax.ShapeDtypeStruct((modes_dim * variables * rows, cols), jnp.float32),
            jax.ShapeDtypeStruct((modes_dim, pod), jnp.float32),
        ),
        in_specs=[VMEM] * 5,
        out_specs=(VMEM, VMEM),
        scratch_shapes=[
            scratch,
            scratch,
            pltpu.VMEM((3, rows + 2, variables, modes_dim, cols), jnp.float32),
            pltpu.VMEM((9 * variables * variables, rows, cols), jnp.float32),
        ],
        compiler_params=pltpu.CompilerParams(vmem_limit_bytes=52 * 1024 * 1024),
    )(
        field,
        scale,
        neighbour_codes,
        jacobian.reshape(jacobian.shape[0], variables * variables, rows, cols),
        pod_basis,
    )
    share = modes_dim // count
    reduced = pl.pallas_call(
        functools.partial(sum_kernel, slabs, crosses),
        out_shape=jax.ShapeDtypeStruct((count, share, pod), jnp.float32),
        in_specs=[VMEM],
        out_specs=VMEM,
        scratch_shapes=[
            pltpu.VMEM((count, share, pod), jnp.float32),
            pltpu.VMEM((share, pod), jnp.float32),
            dma((count,)),
            dma((count,)),
            dma((count,)),
            dma((count,)),
        ],
        compiler_params=pltpu.CompilerParams(collective_id=1, has_side_effects=True),
    )(partial_value.reshape(count, share, pod))
    return (
        induced.reshape(modes_dim, variables, rows, cols),
        reduced.reshape(modes_dim, pod),
    )


def padded_2(block, sides, width):
    for axis, dim in sides:
        count = lax.axis_size(axis)
        forward = [(i, i + 1) for i in range(count - 1)]
        backward = [(target, source) for source, target in forward]
        low = lax.ppermute(
            lax.slice_in_dim(block, block.shape[dim] - width, None, axis=dim), axis, forward
        )
        high = lax.ppermute(lax.slice_in_dim(block, 0, width, axis=dim), axis, backward)
        block = jnp.concatenate([low, block, high], axis=dim)
    return block


def lift_state(lift_gain, field_now):
    accumulated = 0.0
    for component in range(lift_gain.shape[1]):
        accumulated = accumulated + lift_gain[:, component] * jnp.expand_dims(
            field_now[..., component, :, :], -3
        )
    return accumulated


def offset_blocks(codes, jacobian):
    zero_block = jnp.zeros((), jnp.bfloat16)
    stacked = []
    for offset_code in range(9):
        chosen = jnp.where((codes == offset_code)[:, None, None], jacobian, zero_block)
        stacked.append(jnp.sum(chosen, axis=0, dtype=jnp.float32))
    return jnp.stack(stacked)


def apply_blocks(blocks, padded, cell_rows, cell_cols):
    accumulated = 0.0
    for offset_code in range(9):
        start_x = offset_code // 3
        start_y = offset_code % 3
        shifted = padded[..., start_x : start_x + cell_rows, start_y : start_y + cell_cols]
        for component in range(blocks.shape[2]):
            accumulated = accumulated + blocks[offset_code, :, component] * jnp.expand_dims(
                shifted[..., component, :, :], -3
            )
    return accumulated


def body(
    mode_shapes,
    stencil,
    stencil_weight,
    owner_slab,
    target_cell,
    neighbour_codes,
    jacobian,
    lift_matrix,
    pod_basis,
):
    slab_count = lax.axis_size("slab")
    cross_count = lax.axis_size("cross")
    mode_count, space_dims, nodes_dev = mode_shapes.shape
    surf_dev = owner_slab.shape[0]
    capacity = 2 * surf_dev // slab_count
    cell_rows = neighbour_codes.shape[1]
    cell_cols = neighbour_codes.shape[2]
    total_nodes = nodes_dev * slab_count * cross_count
    squares = jnp.sum(mode_shapes * mode_shapes, axis=(1, 2))
    scale_rms = jnp.sqrt(lax.psum(squares, ("slab", "cross")) / (space_dims * total_nodes) + 1e-06)
    shapes_used = mode_shapes / scale_rms[:, None, None]
    picked = shapes_used[:, :, stencil]
    surface = jnp.sum(stencil_weight[None, None] * picked, axis=2)
    dest_slab = owner_slab[:, 0]
    onehot = (dest_slab[:, None] == jnp.arange(slab_count, dtype=jnp.int32)[None, :]).astype(
        jnp.int32
    )
    slot_rank = jnp.sum((jnp.cumsum(onehot, axis=0) - 1) * onehot, axis=1)
    position = dest_slab * capacity + slot_rank
    payload = jnp.zeros((mode_count * space_dims, slab_count * capacity), jnp.float32)
    payload = payload.at[:, position].set(surface.reshape(mode_count * space_dims, surf_dev))
    labels = jnp.zeros((1, slab_count * capacity), jnp.int32).at[0, position].set(target_cell)
    arrived, arrived_cells = (
        lax.all_to_all(payload, "slab", split_axis=1, concat_axis=1, tiled=True),
        lax.all_to_all(labels, "slab", split_axis=1, concat_axis=1, tiled=True),
    )
    deposit = jnp.zeros((mode_count * space_dims, cell_rows * cell_cols), jnp.float32)
    deposit = (
        deposit.at[:, arrived_cells[0]]
        .add(arrived)
        .reshape(mode_count, space_dims, cell_rows, cell_cols)
    )
    rim_width = SWEEPS + 1
    source_padded = padded_2(deposit, (("slab", 2), ("cross", 3)), rim_width)
    grid_x = (
        lax.axis_index("slab") * cell_rows
        - rim_width
        + jnp.arange(cell_rows + 2 * rim_width, dtype=jnp.int32)
    )
    grid_y = (
        lax.axis_index("cross") * cell_cols
        - rim_width
        + jnp.arange(cell_cols + 2 * rim_width, dtype=jnp.int32)
    )
    inside_x = (grid_x >= 0) & (grid_x < cell_rows * slab_count)
    inside_y = (grid_y >= 0) & (grid_y < cell_cols * cross_count)
    inside_mask = (inside_x[:, None] & inside_y[None, :]).astype(jnp.float32)
    field_now = source_padded
    for sweep_index in range(SWEEPS):
        edge_start = sweep_index + 1
        upper_x = cell_rows + 2 * rim_width - edge_start
        upper_y = cell_cols + 2 * rim_width - edge_start
        neighbours = (
            field_now[..., 2:, 1:-1]
            + field_now[..., :-2, 1:-1]
            + field_now[..., 1:-1, 2:]
            + field_now[..., 1:-1, :-2]
        )
        field_now = (
            source_padded[..., edge_start:upper_x, edge_start:upper_y] + SPREAD * neighbours
        ) * inside_mask[edge_start:upper_x, edge_start:upper_y]
    lift_padded = padded_2(lift_matrix, (("slab", 2), ("cross", 3)), 1)
    state_padded = lift_state(lift_padded.astype(jnp.float32), field_now)
    blocks = offset_blocks(neighbour_codes, jacobian)
    induced = apply_blocks(blocks, state_padded, cell_rows, cell_cols)
    partial_value = jnp.dot(
        induced.reshape(mode_count, -1),
        pod_basis.reshape(-1, pod_basis.shape[-1]),
        precision=lax.Precision.HIGHEST,
        preferred_element_type=jnp.float32,
    )
    reduced = lax.psum(partial_value, ("slab", "cross"))
    return (induced, reduced)


def solution(mesh):
    in_specs = (
        P(None, None, ("slab", "cross")),
        P(None, ("slab", "cross")),
        P(None, ("slab", "cross")),
        P(("slab", "cross"), None),
        P(("slab", "cross")),
        P(None, "slab", "cross"),
        P("groups", None, None, "slab", "cross"),
        P("groups", None, "slab", "cross"),
        P("groups", "slab", "cross", None),
    )
    out_specs = (P("groups", None, "slab", "cross"), P("groups", None))
    slabs, crosses = mesh.shape["slab"], mesh.shape["cross"]
    chosen = fast_body if crosses == 2 and slabs == 8 else body
    return jax.shard_map(chosen, mesh=mesh, in_specs=in_specs, out_specs=out_specs, check_vma=False)
```

profile of v0, /device:TPU:0, one launch (start us, length us, event | category | flops | bytes accessed | tf_op | source)
XLA Modules:
  0.0 103.7 jit_solution(16554410103081851135)
XLA Ops:
  0.6 0.9 copy.12
  1.5 0.1 copy.13
  1.6 0.9 pad.8.modes_ref
  2.5 0.0 copy-start.4
  2.5 0.7 copy-done.4
  3.2 0.0 copy-start.5
  3.2 0.7 copy-done.5
  3.9 0.0 copy-start.6
  3.9 0.7 copy-done.6
  4.6 0.0 copy-start.7
  4.6 0.7 copy-done.7
  5.3 27.0 %shard_map.104 = (f32[2,42,112,128]{3,2,1,0:T(8,128)S(1)}, f32[32,128]{1,0:T(8,128)S(1)}) custom-call(f32[128,256]{1,0:T(8,128)S(1)} %pad.8.modes_ref, s32[3,512]{1,0:T(4,128)S(1)} %copy-done.4, f32[3,512]{1,0:T(4,128)S(1)} %copy-done.5, s32[1,512]{1,0:T(1,128)S(1)} %bitcast.14, s32[1,512]{1,0:T(1,128)S(1)} %bitcast.15, ...), custom_call_target="tpu_custom_call" | custom-call | tf_op jit(solution)/shard_map/pallas_call | solution.py:468
  32.3 0.0 copy-start
  32.3 2.1 %copy-done = f32[2,42,112,128]{3,2,1,0:T(8,128)} copy-done((f32[2,42,112,128]{3,2,1,0:T(8,128)}, f32[2,42,112,128]{3,2,1,0:T(8,128)S(1)}, u32[]{:S(2)}) %copy-start) | copy-done | bytes 4816920
  34.5 0.0 copy-start.1
  34.5 1.4 %copy-done.1 = bf16[7,5,5,32,128]{4,3,2,1,0:T(8,128)(2,1)S(1)} copy-done((bf16[7,5,5,32,128]{4,3,2,1,0:T(8,128)(2,1)S(1)}, bf16[7,5,5,32,128]{4,3,2,1,0:T(8,128)(2,1)}, u32[]{:S(2)}) %copy-start.1) | copy-done | bytes 1433624
  35.8 0.0 copy-start.2
  35.8 0.9 copy-done.2
  36.7 49.3 %shard_map.105 = (f32[5120,128]{1,0:T(8,128)}, f32[32,128]{1,0:T(8,128)S(1)}) custom-call(f32[2,42,112,128]{3,2,1,0:T(8,128)} %copy-done, f32[32,128]{1,0:T(8,128)S(1)} %get-tuple-element.7.scale_ref, s32[7,32,128]{2,1,0:T(8,128)S(1)} %copy-done.2, bf16[7,25,32,128]{3,2,1,0:T(8,128)(2,1)S(1)} %bitcast.12, bf16[5,32,128,128]{3,2,1,0:T(8,128)(2,1)} %pod_ref.1), custom_call_target="tpu_custom_call" | custom-call | tf_op jit(solution)/shard_map/pallas_call | solution.py:505
  86.0 0.0 copy-start.3
  86.1 0.6 copy-done.3
  86.7 15.7 %shard_map.106 = f32[16,2,128]{2,1,0:T(2,128)} custom-call(f32[16,2,128]{2,1,0:T(2,128)} %bitcast.13), custom_call_target="tpu_custom_call" | custom-call | tf_op jit(solution)/shard_map/pallas_call | solution.py:528
  102.4 1.3 %copy.15 = f32[32,128]{1,0:T(8,128)} copy(f32[32,128]{1,0:T(8,128)} %bitcast.18) | data formatting | bytes 32768
  (1 shorter events, 0.0 us)
Async XLA Ops:
  2.5 0.7 copy-start.4
  3.2 0.7 copy-start.5
  3.9 0.7 copy-start.6
  4.6 0.7 copy-start.7
  32.3 2.2 %copy-start = (f32[2,42,112,128]{3,2,1,0:T(8,128)}, f32[2,42,112,128]{3,2,1,0:T(8,128)S(1)}, u32[]{:S(2)}) copy-start(f32[2,42,112,128]{3,2,1,0:T(8,128)S(1)} %get-tuple-element.6.field_ref) | copy-start | bytes 14450692
  34.5 1.4 %copy-start.1 = (bf16[7,5,5,32,128]{4,3,2,1,0:T(8,128)(2,1)S(1)}, bf16[7,5,5,32,128]{4,3,2,1,0:T(8,128)(2,1)}, u32[]{:S(2)}) copy-start(bf16[7,5,5,32,128]{4,3,2,1,0:T(8,128)(2,1)} %param.15) | copy-start | bytes 4300804
  35.8 0.9 copy-start.2
  86.0 0.6 copy-start.3
where the time goes:
time: 104 us
  Pallas kernels  92.1 us (89%)
  local copies, waits for them, and re-layouts  11 us (11%)
    pallas_call x1, Pallas kernels, fast_body(): pl.pallas_call(functools.partial(local_kernel, slabs, rows, modes_dim, co...  49.3 us
    pallas_call x1, Pallas kernels, fast_body(): pl.pallas_call(functools.partial(route_kernel, slabs, rows, modes_dim, co...  27 us
    pallas_call x1, Pallas kernels, fast_body(): pl.pallas_call(functools.partial(sum_kernel, slabs, crosses), out_shape=j...  15.7 us
    unnamed x18, local copies, waits for them, and re-layouts  9.99 us

commit v1 on v0

--- a/solution.py
+++ b/solution.py
@@ -27,18 +27,33 @@
     return high, low
 
 
-def route_kernel(
+def whole_kernel(
     slabs,
     rows,
     modes_dim,
     comps,
+    variables,
     node_total,
-    modes_ref,
+    shapes_hbm,
+    stencil_hbm,
+    weight_hbm,
+    owner_hbm,
+    target_hbm,
+    lift_hbm,
+    codes_hbm,
+    jac_hbm,
+    pod_hbm,
+    induced_hbm,
+    reduced_ref,
     stencil_ref,
     weight_ref,
     owner_ref,
     target_ref,
     lift_ref,
+    codes_ref,
+    jac_ref,
+    pod_ref,
+    modes_ref,
     field_ref,
     scale_ref,
     send_buf,
@@ -46,6 +61,18 @@
     arrived,
     labels,
     squares,
+    ping,
+    pong,
+    state,
+    blocks,
+    pending,
+    induced_ref,
+    part_ref,
+    got,
+    mine_sum,
+    sum_ref,
+    fetch_sem,
+    out_sem,
     send_sem,
     recv_sem,
     edge_send,
@@ -54,20 +81,50 @@
     pair_recv,
     sq_send,
     sq_recv,
+    part_send,
+    part_recv,
+    back_send,
+    back_recv,
 ):
     me = lax.axis_index("slab")
     mine = lax.axis_index("cross")
     other = 1 - mine
     nodes = modes_ref.shape[1]
+    count = 2 * slabs
+    data = modes_dim * comps
+    rank_here = me * 2 + mine
     surf = stencil_ref.shape[1]
-    data = modes_dim * comps
+
+    fetched = [
+        pltpu.make_async_copy(source, held, fetch_sem.at[n])
+        for n, (source, held) in enumerate(
+            (
+                (shapes_hbm, modes_ref.at[pl.ds(0, data)]),
+                (stencil_hbm, stencil_ref),
+                (weight_hbm, weight_ref),
+                (owner_hbm, owner_ref),
+                (target_hbm, target_ref),
+                (lift_hbm, lift_ref),
+                (codes_hbm, codes_ref),
+                (jac_hbm, jac_ref),
+                (pod_hbm, pod_ref),
+            )
+        )
+    ]
+    for copy in fetched:
+        copy.start()
+
+    def peer(k):
+        at = lax.rem(rank_here + k, count)
+        return at, {"slab": lax.div(at, 2), "cross": lax.rem(at, 2)}
 
     barrier = pltpu.get_barrier_semaphore()
-    for k in range(1, slabs):
-        pl.semaphore_signal(
-            barrier, inc=1, device_id={"slab": lax.rem(me + k, slabs)}, device_id_type=MESH
-        )
-    pl.semaphore_signal(barrier, inc=1, device_id={"cross": other}, device_id_type=MESH)
+    for k in range(1, count):
+        pl.semaphore_signal(barrier, inc=1, device_id=peer(k)[1], device_id_type=MESH)
+
+    for copy in fetched[0:6]:
+        copy.wait()
+    modes_ref[data:, :] = jnp.zeros((LANES - data, nodes), jnp.float32)
 
     node_id = lax.broadcasted_iota(jnp.int32, (nodes, surf), 0)
     mix = jnp.zeros((nodes, surf), jnp.float32)
@@ -107,7 +164,7 @@
     out_rows = send_buf.shape[1]
     out_id = lax.broadcasted_iota(jnp.int32, (out_rows, LANES), 0)
 
-    pl.semaphore_wait(barrier, slabs)
+    pl.semaphore_wait(barrier, count - 1)
     copies = []
     for step in range(slabs):
         k = (step + 1) % slabs
@@ -133,7 +190,14 @@
             copy.start()
             copies.append(copy)
 
-    field_ref[mine, RIM : RIM + rows, data:, :] = lift_ref[...]
+    for comp in range(comps):
+        for b in range(variables):
+            field_ref[mine, RIM : RIM + rows, data + comp * variables + b, :] = lift_ref[
+                b, comp
+            ].astype(jnp.float32)
+    field_ref[mine, RIM : RIM + rows, data + comps * variables, :] = jnp.zeros(
+        (rows, LANES), jnp.float32
+    )
 
     @pl.when(me == 0)
     def _():
@@ -142,6 +206,23 @@
     @pl.when(me == slabs - 1)
     def _():
         field_ref[mine, RIM + rows :] = jnp.zeros((RIM,) + field_ref.shape[2:], jnp.float32)
+
+    for copy in fetched[6:8]:
+        copy.wait()
+    square = variables * variables
+
+    def select(pair, carry):
+        for x0 in range(0, rows, 8):
+            chosen = [jac_ref[k, pair, x0 : x0 + 8, :].astype(jnp.float32) for k in range(7)]
+            codes = [codes_ref[k, x0 : x0 + 8, :] for k in range(7)]
+            for code in range(9):
+                value = jnp.zeros((8, LANES), jnp.float32)
+                for k in range(7):
+                    value = jnp.where(codes[k] == code, chosen[k], value)
+                blocks[code * square + pair, x0 : x0 + 8, :] = value
+        return carry
+
+    lax.fori_loop(0, square, select, 0)
 
     total = square_row
     for k in range(slabs):
@@ -248,61 +329,13 @@
     inverse = 1.0 / jnp.sqrt(per_mode / node_total + 1e-06)
     scale_ref[...] = jnp.broadcast_to(inverse, scale_ref.shape)
 
-    for copy in copies:
-        copy.wait_send()
-
-    @pl.when(me < slabs - 1)
-    def _():
-        up.wait_send()
-
-    @pl.when(me > 0)
-    def _():
-        down.wait_send()
-
     middle.wait()
     low_rim.wait()
     high_rim.wait()
 
-
-def local_kernel(
-    slabs,
-    rows,
-    modes_dim,
-    comps,
-    variables,
-    field_ref,
-    scale_ref,
-    codes_ref,
-    jac_ref,
-    pod_ref,
-    induced_ref,
-    partial_ref,
-    ping,
-    pong,
-    state,
-    blocks,
-):
-    me = lax.axis_index("slab")
-    mine = lax.axis_index("cross")
-    other = 1 - mine
-    data = modes_dim * comps
     planes = rows + 2 * RIM
     lane = lax.broadcasted_iota(jnp.int32, (modes_dim, LANES), 1)
     first, last = lane == 0, lane == LANES - 1
-    square = variables * variables
-
-    def select(pair, carry):
-        for x0 in range(0, rows, 8):
-            chosen = [jac_ref[k, pair, x0 : x0 + 8, :].astype(jnp.float32) for k in range(7)]
-            codes = [codes_ref[k, x0 : x0 + 8, :] for k in range(7)]
-            for code in range(9):
-                value = jnp.zeros((8, LANES), jnp.float32)
-                for k in range(7):
-                    value = jnp.where(codes[k] == code, chosen[k], value)
-                blocks[code * square + pair, x0 : x0 + 8, :] = value
-        return carry
-
-    lax.fori_loop(0, square, select, 0)
 
     def sweep(source, result, edge):
         def plane(x, carry):
@@ -323,7 +356,7 @@
                     ) * inside
             return carry
 
-        lax.fori_loop(edge, planes - edge, plane, 0)
+        lax.fori_loop(edge, planes - edge, plane, 0, unroll=2)
 
     sweep(field_ref, ping, 1)
     sweep(ping, pong, 2)
@@ -351,11 +384,21 @@
             )
         return carry
 
-    lax.fori_loop(0, rows + 2, lift, 0)
+    lax.fori_loop(0, rows + 2, lift, 0, unroll=2)
 
     stride = variables * rows
 
+    def project(x, total):
+        for b in range(variables):
+            total = total + jnp.dot(
+                pending[:, b * LANES : (b + 1) * LANES],
+                pod_ref[b, x],
+                preferred_element_type=jnp.float32,
+            )
+        return total
+
     def apply(x, total):
+        total = project(jnp.maximum(x - 1, 0), total)
         sums = [jnp.zeros((modes_dim, LANES), jnp.float32) for _ in range(variables)]
         for code in range(9):
             for a in range(variables):
@@ -367,58 +410,47 @@
             result = sums[b] * scale_ref[...]
             induced_ref[pl.ds(b * rows + x, modes_dim, stride=stride), :] = result
             high, low = split_2(result)
-            total = total + jnp.dot(
-                jnp.concatenate([high, low], axis=0),
-                pod_ref[b, x],
-                preferred_element_type=jnp.float32,
-            )
+            pending[0:modes_dim, b * LANES : (b + 1) * LANES] = high
+            pending[modes_dim:, b * LANES : (b + 1) * LANES] = low
         return total
 
+    fetched[8].wait()
+    pending[...] = jnp.zeros(pending.shape, jnp.bfloat16)
     total = lax.fori_loop(
-        0, rows, apply, jnp.zeros((2 * modes_dim, partial_ref.shape[1]), jnp.float32)
-    )
-    partial_ref[...] = total[0:modes_dim] + total[modes_dim:]
-
-
-def sum_kernel(
-    slabs, crosses, part_ref, out_ref, got, mine_sum, send_sem, recv_sem, back_send, back_recv
-):
-    me = lax.axis_index("slab") * crosses + lax.axis_index("cross")
-    count = slabs * crosses
-
-    def peer(k):
-        at = lax.rem(me + k, count)
-        return at, {"slab": lax.div(at, crosses), "cross": lax.rem(at, crosses)}
-
-    barrier = pltpu.get_barrier_semaphore()
-    for k in range(1, count):
-        pl.semaphore_signal(barrier, inc=1, device_id=peer(k)[1], device_id_type=MESH)
-    pl.semaphore_wait(barrier, count - 1)
-    copies = []
+        0, rows, apply, jnp.zeros((2 * modes_dim, reduced_ref.shape[1]), jnp.float32)
+    )
+    total = project(rows - 1, total)
+    result = total[0:modes_dim] + total[modes_dim:]
+    share = modes_dim // count
+    for n in range(count):
+        part_ref[n] = result[n * share : (n + 1) * share]
+    written = pltpu.make_async_copy(induced_ref, induced_hbm, out_sem)
+    written.start()
+    parts = []
     for k in range(1, count):
         at, device = peer(k)
         copy = pltpu.make_async_remote_copy(
             src_ref=part_ref.at[at],
             dst_ref=got.at[k],
-            send_sem=send_sem.at[k],
-            recv_sem=recv_sem.at[k],
+            send_sem=part_send.at[k],
+            recv_sem=part_recv.at[k],
             device_id=device,
             device_id_type=MESH,
         )
         copy.start()
-        copies.append(copy)
-    total = part_ref[me]
+        parts.append(copy)
+    total = part_ref[rank_here]
     for k in range(1, count):
-        copies[k - 1].wait_recv()
+        parts[k - 1].wait_recv()
         total = total + got[k]
     mine_sum[...] = total
-    out_ref[me] = total
+    sum_ref[rank_here] = total
     backs = []
     for k in range(1, count):
-        at, device = peer(k)
+        _, device = peer(k)
         copy = pltpu.make_async_remote_copy(
             src_ref=mine_sum,
-            dst_ref=out_ref.at[me],
+            dst_ref=sum_ref.at[rank_here],
             send_sem=back_send.at[k],
             recv_sem=back_recv.at[k],
             device_id=device,
@@ -426,13 +458,28 @@
         )
         copy.start()
         backs.append(copy)
-    for copy in copies:
+    for copy in parts:
         copy.wait_send()
     for copy in backs:
         copy.wait()
+    for n in range(count):
+        reduced_ref[n * share : (n + 1) * share, :] = sum_ref[n]
+    for copy in copies:
+        copy.wait_send()
+
+    @pl.when(me < slabs - 1)
+    def _():
+        up.wait_send()
+
+    @pl.when(me > 0)
+    def _():
+        down.wait_send()
+    written.wait()
 
 
 VMEM = pl.BlockSpec(memory_space=pltpu.VMEM)
+
+ANY = pl.BlockSpec(memory_space=pl.ANY)
 
 
 def fast_body(
@@ -454,33 +501,60 @@
     variables = lift_matrix.shape[0]
     pod = pod_basis.shape[-1]
     data = modes_dim * comps
-    lift_rows = 16
     planes = rows + 2 * RIM
     count = slabs * crosses
-    modes = jnp.pad(
-        mode_shapes.transpose(1, 0, 2).reshape(data, nodes), ((0, LANES - data), (0, 0))
-    )
-    lift = jnp.pad(
-        lift_matrix.transpose(2, 1, 0, 3).reshape(rows, comps * variables, cols),
-        ((0, 0), (0, lift_rows - comps * variables), (0, 0)),
-    ).astype(jnp.float32)
+    share = modes_dim // count
     dma = pltpu.SemaphoreType.DMA
-    field, scale = pl.pallas_call(
+    operands = (
+        mode_shapes.transpose(1, 0, 2).reshape(data, nodes),
+        stencil,
+        stencil_weight,
+        owner_slab.reshape(1, surf),
+        target_cell.reshape(1, surf),
+        lift_matrix,
+        neighbour_codes,
+        jacobian.reshape(jacobian.shape[0], variables * variables, rows, cols),
+        pod_basis,
+    )
+    sweep_shape = pltpu.VMEM((crosses, planes, data, cols), jnp.float32)
+    induced, reduced = pl.pallas_call(
         functools.partial(
-            route_kernel, slabs, rows, modes_dim, comps, float(comps * nodes * count)
+            whole_kernel,
+            slabs,
+            rows,
+            modes_dim,
+            comps,
+            variables,
+            float(comps * nodes * count),
         ),
         out_shape=(
-            jax.ShapeDtypeStruct((crosses, planes, data + lift_rows, cols), jnp.float32),
-            jax.ShapeDtypeStruct((modes_dim, LANES), jnp.float32),
+            jax.ShapeDtypeStruct((modes_dim * variables * rows, cols), jnp.float32),
+            jax.ShapeDtypeStruct((modes_dim, pod), jnp.float32),
         ),
-        in_specs=[VMEM] * 6,
-        out_specs=(VMEM, VMEM),
-        scratch_shapes=[
+        in_specs=[ANY] * len(operands),
+        out_specs=(ANY, VMEM),
+        scratch_shapes=[pltpu.VMEM(x.shape, x.dtype) for x in operands[1:]]
+        + [
+            pltpu.VMEM((LANES, nodes), jnp.float32),
+            pltpu.VMEM((crosses, planes, data + 16, cols), jnp.float32),
+            pltpu.VMEM((modes_dim, LANES), jnp.float32),
             pltpu.VMEM((slabs, data + 8, LANES), jnp.float32),
             pltpu.VMEM((slabs, data + 8, LANES), jnp.float32),
             pltpu.VMEM((2 * data, slabs * LANES), jnp.bfloat16),
             pltpu.VMEM((8, slabs * LANES), jnp.int32),
             pltpu.VMEM((2, 8, LANES), jnp.float32),
+            sweep_shape,
+            sweep_shape,
+            pltpu.VMEM((3, rows + 2, variables, modes_dim, cols), jnp.float32),
+            pltpu.VMEM((9 * variables * variables, rows, cols), jnp.float32),
+            pltpu.VMEM((2 * modes_dim, variables * cols), jnp.bfloat16),
+            pltpu.VMEM((modes_dim * variables * rows, cols), jnp.float32),
+            pltpu.VMEM((count, share, pod), jnp.float32),
+            pltpu.VMEM((count, share, pod), jnp.float32),
+            pltpu.VMEM((share, pod), jnp.float32),
+            pltpu.VMEM((count, share, pod), jnp.float32),
+            dma((len(operands),)),
+            dma,
             dma((slabs,)),
             dma((slabs,)),
             dma((2,)),
@@ -489,61 +563,16 @@
             dma((3,)),
             dma,
             dma,
-        ],
-        compiler_params=pltpu.CompilerParams(
-            collective_id=0, has_side_effects=True, vmem_limit_bytes=40 * 1024 * 1024
-        ),
-    )(
-        modes,
-        stencil,
-        stencil_weight,
-        owner_slab.reshape(1, surf),
-        target_cell.reshape(1, surf),
-        lift,
-    )
-    scratch = pltpu.VMEM((crosses, planes, data, cols), jnp.float32)
-    induced, partial_value = pl.pallas_call(
-        functools.partial(local_kernel, slabs, rows, modes_dim, comps, variables),
-        out_shape=(
-            jax.ShapeDtypeStruct((modes_dim * variables * rows, cols), jnp.float32),
-            jax.ShapeDtypeStruct((modes_dim, pod), jnp.float32),
-        ),
-        in_specs=[VMEM] * 5,
-        out_specs=(VMEM, VMEM),
-        scratch_shapes=[
-            scratch,
-            scratch,
-            pltpu.VMEM((3, rows + 2, variables, modes_dim, cols), jnp.float32),
-            pltpu.VMEM((9 * variables * variables, rows, cols), jnp.float32),
-        ],
-        compiler_params=pltpu.CompilerParams(vmem_limit_bytes=52 * 1024 * 1024),
-    )(
-        field,
-        scale,
-        neighbour_codes,
-        jacobian.reshape(jacobian.shape[0], variables * variables, rows, cols),
-        pod_basis,
-    )
-    share = modes_dim // count
-    reduced = pl.pallas_call(
-        functools.partial(sum_kernel, slabs, crosses),
-        out_shape=jax.ShapeDtypeStruct((count, share, pod), jnp.float32),
-        in_specs=[VMEM],
-        out_specs=VMEM,
-        scratch_shapes=[
-            pltpu.VMEM((count, share, pod), jnp.float32),
-            pltpu.VMEM((share, pod), jnp.float32),
             dma((count,)),
             dma((count,)),
             dma((count,)),
             dma((count,)),
         ],
-        compiler_params=pltpu.CompilerParams(collective_id=1, has_side_effects=True),
-    )(partial_value.reshape(count, share, pod))
-    return (
-        induced.reshape(modes_dim, variables, rows, cols),
-        reduced.reshape(modes_dim, pod),
-    )
+        compiler_params=pltpu.CompilerParams(
+            collective_id=0, has_side_effects=True, vmem_limit_bytes=56 * 1024 * 1024
+        ),
+    )(*operands)
+    return induced.reshape(modes_dim, variables, rows, cols), reduced
 
 
 def padded_2(block, sides, width):

time: 104 us -> 79 us (0.76)
  Pallas kernels: 92.1 us -> 74.1 us
  local copies, waits for them, and re-layouts: 11 us -> 4.1 us
    pallas_call x3 -> x1, Pallas kernels: 92.1 us -> 74.1 us  [fast_body(): pl.pallas_call(functools.partial(whole_kernel, slabs, rows, modes_dim, co...]
    unnamed x18 -> x4, local copies, waits for them, and re-layouts: 9.99 us -> 4.1 us
where the time goes in v1:
time: 79 us; the launch traced here: 78.8 us
  Pallas kernels  74.1 us (94%)
  local copies, waits for them, and re-layouts  4.1 us (5%)
    pallas_call x1, Pallas kernels, fast_body(): pl.pallas_call(functools.partial(whole_kernel, slabs, rows, modes_dim, co...  74.1 us
    unnamed x4, local copies, waits for them, and re-layouts  4.1 us

profile of v1, /device:TPU:0, one launch (start us, length us, event | category | flops | bytes accessed | tf_op | source)
XLA Modules:
  0.0 78.8 jit_solution(9139120740676746355)
XLA Ops:
  0.6 74.1 %shard_map.104 = (f32[5120,128]{1,0:T(8,128)}, f32[32,128]{1,0:T(8,128)}) custom-call(f32[96,256]{1,0:T(8,128)} %bitcast.9, s32[3,512]{1,0:T(4,128)} %stencil_hbm.1, f32[3,512]{1,0:T(4,128)} %weight_hbm.1, s32[1,512]{1,0:T(1,128)} %bitcast.10, s32[1,512]{1,0:T(1,128)} %bitcast.11, bf16[5,3,32,128]{3,2,1,0:T(8,128)(2,1)} %lift_hbm.1, ...), custom_call_target="tpu_custom_call" | custom-call | tf_op jit(solution)/shard_map/pallas_call | solution.py:520
  74.7 0.0 copy-start
  74.7 3.5 %copy.13 = f32[32,5,32,128]{3,2,1,0:T(8,128)} copy(f32[32,5,32,128]{3,2,1,0:T(8,128)} %bitcast.7) | data formatting | bytes 5242880
  78.2 0.0 copy-done
  78.2 0.6 copy.14
Async XLA Ops:
  74.7 3.5 %copy-start = (f32[32,128]{1,0:T(8,128)S(1)}, f32[32,128]{1,0:T(8,128)}, u32[]{:S(2)}) copy-start(f32[32,128]{1,0:T(8,128)} %get-tuple-element.9) | copy-start | bytes 49156

commit v2 on v1

--- a/solution.py
+++ b/solution.py
@@ -43,7 +43,7 @@
     codes_hbm,
     jac_hbm,
     pod_hbm,
-    induced_hbm,
+    induced_ref,
     reduced_ref,
     stencil_ref,
     weight_ref,
@@ -61,18 +61,19 @@
     arrived,
     labels,
     squares,
-    ping,
-    pong,
+    field_1,
+    field_2,
+    field_3,
+    field_4,
     state,
     blocks,
     pending,
-    induced_ref,
     part_ref,
+    pair_part,
+    chip_sum,
     got,
-    mine_sum,
     sum_ref,
     fetch_sem,
-    out_sem,
     send_sem,
     recv_sem,
     edge_send,
@@ -90,9 +91,7 @@
     mine = lax.axis_index("cross")
     other = 1 - mine
     nodes = modes_ref.shape[1]
-    count = 2 * slabs
     data = modes_dim * comps
-    rank_here = me * 2 + mine
     surf = stencil_ref.shape[1]
 
     fetched = [
@@ -114,13 +113,12 @@
     for copy in fetched:
         copy.start()
 
-    def peer(k):
-        at = lax.rem(rank_here + k, count)
-        return at, {"slab": lax.div(at, 2), "cross": lax.rem(at, 2)}
-
     barrier = pltpu.get_barrier_semaphore()
-    for k in range(1, count):
-        pl.semaphore_signal(barrier, inc=1, device_id=peer(k)[1], device_id_type=MESH)
+    for k in range(1, slabs):
+        pl.semaphore_signal(
+            barrier, inc=1, device_id={"slab": lax.rem(me + k, slabs)}, device_id_type=MESH
+        )
+    pl.semaphore_signal(barrier, inc=1, device_id={"cross": other}, device_id_type=MESH)
 
     for copy in fetched[0:6]:
         copy.wait()
@@ -164,7 +162,7 @@
     out_rows = send_buf.shape[1]
     out_id = lax.broadcasted_iota(jnp.int32, (out_rows, LANES), 0)
 
-    pl.semaphore_wait(barrier, count - 1)
+    pl.semaphore_wait(barrier, slabs)
     copies = []
     for step in range(slabs):
         k = (step + 1) % slabs
@@ -286,9 +284,15 @@
             device_id_type=MESH,
         )
 
-    middle = across(0, RIM, rows)
-    low_rim = across(1, 0, RIM)
-    high_rim = across(2, RIM + rows, RIM)
+    third = (pairs - 6) // 2
+    middle = [
+        across(0, RIM + rows - 6, 6),
+        across(1, RIM, 6),
+        across(2, RIM + 6, 2 * third),
+        across(3, RIM + 6 + 2 * third, rows - 12 - 2 * third),
+    ]
+    low_rim = across(4, 0, RIM)
+    high_rim = across(5, RIM + rows, RIM)
 
     lax.fori_loop(0, 3, deposit, 0)
 
@@ -296,26 +300,18 @@
     def _():
         up.start()
 
+    middle[0].start()
     lax.fori_loop(3, 6, deposit, 0)
 
     @pl.when(me > 0)
     def _():
         down.start()
 
-    lax.fori_loop(6, pairs, deposit, 0)
-    middle.start()
-
-    @pl.when(me > 0)
-    def _():
-        up.wait_recv()
-
-    low_rim.start()
-
-    @pl.when(me < slabs - 1)
-    def _():
-        down.wait_recv()
-
-    high_rim.start()
+    middle[1].start()
+    lax.fori_loop(6, 6 + third, deposit, 0)
+    middle[2].start()
+    lax.fori_loop(6 + third, pairs, deposit, 0)
+    middle[3].start()
 
     sq_copy.wait()
     whole = squares[0, 0:1] + squares[1, 0:1]
@@ -329,39 +325,67 @@
     inverse = 1.0 / jnp.sqrt(per_mode / node_total + 1e-06)
     scale_ref[...] = jnp.broadcast_to(inverse, scale_ref.shape)
 
-    middle.wait()
-    low_rim.wait()
-    high_rim.wait()
-
     planes = rows + 2 * RIM
     lane = lax.broadcasted_iota(jnp.int32, (modes_dim, LANES), 1)
     first, last = lane == 0, lane == LANES - 1
 
-    def sweep(source, result, edge):
+    def sweep(source, result, x, inside):
+        for comp in range(comps):
+            part = pl.ds(comp * modes_dim, modes_dim)
+            left, right = source[0, x, part, :], source[1, x, part, :]
+            near_left = pltpu.roll(jnp.where(last, 0.0, left), 1, 1) + pltpu.roll(
+                jnp.where(first, right, left), LANES - 1, 1
+            )
+            near_right = pltpu.roll(jnp.where(last, left, right), 1, 1) + pltpu.roll(
+                jnp.where(first, 0.0, right), LANES - 1, 1
+            )
+            for tile, near in ((0, near_left), (1, near_right)):
+                near = near + source[tile, x - 1, part, :] + source[tile, x + 1, part, :]
+                value = field_ref[tile, x, part, :] + SPREAD * near
+                result[tile, x, part, :] = value if inside is None else value * inside
+
+    fields = [field_1, field_2, field_3, field_4]
+    stages = [field_ref, *fields]
+
+    def inner(step):
         def plane(x, carry):
-            at = x - RIM + me * rows
-            inside = ((at >= 0) & (at < slabs * rows)).astype(jnp.float32)
-            for comp in range(comps):
-                part = pl.ds(comp * modes_dim, modes_dim)
-                left, right = source[0, x, part, :], source[1, x, part, :]
-                left_up, right_up = pltpu.roll(left, 1, 1), pltpu.roll(right, 1, 1)
-                left_down = pltpu.roll(left, LANES - 1, 1)
-                right_down = pltpu.roll(right, LANES - 1, 1)
-                near_left = jnp.where(first, 0.0, left_up) + jnp.where(last, right_down, left_down)
-                near_right = jnp.where(first, left_up, right_up) + jnp.where(last, 0.0, right_down)
-                for tile, near in ((0, near_left), (1, near_right)):
-                    near = near + source[tile, x - 1, part, :] + source[tile, x + 1, part, :]
-                    result[tile, x, part, :] = (
-                        field_ref[tile, x, part, :] + SPREAD * near
-                    ) * inside
+            sweep(stages[step - 1], stages[step], x, None)
             return carry
 
-        lax.fori_loop(edge, planes - edge, plane, 0, unroll=2)
-
-    sweep(field_ref, ping, 1)
-    sweep(ping, pong, 2)
-    sweep(pong, ping, 3)
-    sweep(ping, pong, 4)
+        lax.fori_loop(RIM + step, RIM + rows - step, plane, 0, unroll=2)
+
+    def outer(step):
+        def plane(i, carry):
+            for x in (step + i, planes - RIM - step + i):
+                at = x - RIM + me * rows
+                inside = ((at >= 0) & (at < slabs * rows)).astype(jnp.float32)
+                sweep(stages[step - 1], stages[step], x, inside)
+            return carry
+
+        lax.fori_loop(0, RIM, plane, 0)
+
+    for copy in middle:
+        copy.wait_recv()
+    for step in range(1, SWEEPS):
+        inner(step)
+
+    @pl.when(me > 0)
+    def _():
+        up.wait_recv()
+
+    low_rim.start()
+
+    @pl.when(me < slabs - 1)
+    def _():
+        down.wait_recv()
+
+    high_rim.start()
+    inner(SWEEPS)
+    low_rim.wait_recv()
+    high_rim.wait_recv()
+    for step in range(1, SWEEPS + 1):
+        outer(step)
+    pong = fields[SWEEPS - 1]
 
     here = (mine == 0).astype(jnp.float32)
     there = 1.0 - here
@@ -378,10 +402,8 @@
                     far + field_ref[other, x + RIM - 1, row, :] * pong[other, x + RIM - 1, part, :]
                 )
             state[1, x, b] = own
-            state[0, x, b] = jnp.where(first, pltpu.roll(far, 1, 1) * there, pltpu.roll(own, 1, 1))
-            state[2, x, b] = jnp.where(
-                last, pltpu.roll(far, LANES - 1, 1) * here, pltpu.roll(own, LANES - 1, 1)
-            )
+            state[0, x, b] = pltpu.roll(jnp.where(last, far * there, own), 1, 1)
+            state[2, x, b] = pltpu.roll(jnp.where(first, far * here, own), LANES - 1, 1)
         return carry
 
     lax.fori_loop(0, rows + 2, lift, 0, unroll=2)
@@ -417,53 +439,59 @@
     fetched[8].wait()
     pending[...] = jnp.zeros(pending.shape, jnp.bfloat16)
     total = lax.fori_loop(
-        0, rows, apply, jnp.zeros((2 * modes_dim, reduced_ref.shape[1]), jnp.float32)
+        0, rows, apply, jnp.zeros((2 * modes_dim, reduced_ref.shape[1]), jnp.float32), unroll=2
     )
     total = project(rows - 1, total)
     result = total[0:modes_dim] + total[modes_dim:]
-    share = modes_dim // count
-    for n in range(count):
-        part_ref[n] = result[n * share : (n + 1) * share]
-    written = pltpu.make_async_copy(induced_ref, induced_hbm, out_sem)
-    written.start()
+    half = modes_dim // 2
+    part_ref[0] = result[0:half]
+    part_ref[1] = result[half:]
+    to_pair = pltpu.make_async_remote_copy(
+        src_ref=part_ref.at[other],
+        dst_ref=pair_part,
+        send_sem=back_send.at[0],
+        recv_sem=back_recv.at[0],
+        device_id={"cross": other},
+        device_id_type=MESH,
+    )
+    to_pair.start()
+    to_pair.wait()
+    chip_sum[...] = part_ref[mine] + pair_part[...]
     parts = []
-    for k in range(1, count):
-        at, device = peer(k)
+    for k in range(1, slabs):
         copy = pltpu.make_async_remote_copy(
-            src_ref=part_ref.at[at],
-            dst_ref=got.at[k],
+            src_ref=chip_sum,
+            dst_ref=got.at[me],
             send_sem=part_send.at[k],
             recv_sem=part_recv.at[k],
-            device_id=device,
+            device_id={"slab": lax.rem(me + k, slabs)},
             device_id_type=MESH,
         )
         copy.start()
         parts.append(copy)
-    total = part_ref[rank_here]
-    for k in range(1, count):
-        parts[k - 1].wait_recv()
-        total = total + got[k]
-    mine_sum[...] = total
-    sum_ref[rank_here] = total
-    backs = []
-    for k in range(1, count):
-        _, device = peer(k)
-        copy = pltpu.make_async_remote_copy(
-            src_ref=mine_sum,
-            dst_ref=sum_ref.at[rank_here],
-            send_sem=back_send.at[k],
-            recv_sem=back_recv.at[k],
-            device_id=device,
-            device_id_type=MESH,
-        )
-        copy.start()
-        backs.append(copy)
+    got[me] = chip_sum[...]
     for copy in parts:
+        copy.wait()
+    whole_sum = got[0]
+    for n in range(1, slabs):
+        whole_sum = whole_sum + got[n]
+    sum_ref[mine] = whole_sum
+    back = pltpu.make_async_remote_copy(
+        src_ref=sum_ref.at[mine],
+        dst_ref=sum_ref.at[mine],
+        send_sem=back_send.at[1],
+        recv_sem=back_recv.at[1],
+        device_id={"cross": other},
+        device_id_type=MESH,
+    )
+    back.start()
+    back.wait()
+    reduced_ref[0:half, :] = sum_ref[0]
+    reduced_ref[half:, :] = sum_ref[1]
+    for copy in middle:
         copy.wait_send()
-    for copy in backs:
-        copy.wait()
-    for n in range(count):
-        reduced_ref[n * share : (n + 1) * share, :] = sum_ref[n]
+    low_rim.wait_send()
+    high_rim.wait_send()
     for copy in copies:
         copy.wait_send()
 
@@ -474,7 +502,6 @@
     @pl.when(me > 0)
     def _():
         down.wait_send()
-    written.wait()
 
 
 VMEM = pl.BlockSpec(memory_space=pltpu.VMEM)
@@ -503,7 +530,7 @@
     data = modes_dim * comps
     planes = rows + 2 * RIM
     count = slabs * crosses
-    share = modes_dim // count
+    half = modes_dim // 2
     dma = pltpu.SemaphoreType.DMA
     operands = (
         mode_shapes.transpose(1, 0, 2).reshape(data, nodes),
@@ -532,7 +559,7 @@
             jax.ShapeDtypeStruct((modes_dim, pod), jnp.float32),
         ),
         in_specs=[ANY] * len(operands),
-        out_specs=(ANY, VMEM),
+        out_specs=(VMEM, VMEM),
         scratch_shapes=[pltpu.VMEM(x.shape, x.dtype) for x in operands[1:]]
         + [
             pltpu.VMEM((LANES, nodes), jnp.float32),
@@ -545,28 +572,29 @@
             pltpu.VMEM((2, 8, LANES), jnp.float32),
             sweep_shape,
             sweep_shape,
+            sweep_shape,
+            sweep_shape,
             pltpu.VMEM((3, rows + 2, variables, modes_dim, cols), jnp.float32),
             pltpu.VMEM((9 * variables * variables, rows, cols), jnp.float32),
             pltpu.VMEM((2 * modes_dim, variables * cols), jnp.bfloat16),
-            pltpu.VMEM((modes_dim * variables * rows, cols), jnp.float32),
-            pltpu.VMEM((count, share, pod), jnp.float32),
-            pltpu.VMEM((count, share, pod), jnp.float32),
-            pltpu.VMEM((share, pod), jnp.float32),
-            pltpu.VMEM((count, share, pod), jnp.float32),
+            pltpu.VMEM((2, half, pod), jnp.float32),
+            pltpu.VMEM((half, pod), jnp.float32),
+            pltpu.VMEM((half, pod), jnp.float32),
+            pltpu.VMEM((slabs, half, pod), jnp.float32),
+            pltpu.VMEM((2, half, pod), jnp.float32),
             dma((len(operands),)),
+            dma((slabs,)),
+            dma((slabs,)),
+            dma((2,)),
+            dma((2,)),
+            dma((6,)),
+            dma((6,)),
+            dma,
             dma,
             dma((slabs,)),
             dma((slabs,)),
             dma((2,)),
             dma((2,)),
-            dma((3,)),
-            dma((3,)),
-            dma,
-            dma,
-            dma((count,)),
-            dma((count,)),
-            dma((count,)),
-            dma((count,)),
         ],
         compiler_params=pltpu.CompilerParams(
             collective_id=0, has_side_effects=True, vmem_limit_bytes=56 * 1024 * 1024

time: 79 us -> 66.5 us (0.84)
  Pallas kernels: 74.1 us -> 61.6 us
    pallas_call x1, Pallas kernels: 74.1 us -> 61.6 us  [fast_body(): pl.pallas_call(functools.partial(whole_kernel, slabs, rows, modes_dim, co...]
where the time goes in v2:
time: 66.5 us; the launch traced here: 66.3 us
  Pallas kernels  61.6 us (93%)
  local copies, waits for them, and re-layouts  4.1 us (6%)
    pallas_call x1, Pallas kernels, fast_body(): pl.pallas_call(functools.partial(whole_kernel, slabs, rows, modes_dim, co...  61.6 us
    unnamed x4, local copies, waits for them, and re-layouts  4.1 us

profile of v2, /device:TPU:0, one launch (start us, length us, event | category | flops | bytes accessed | tf_op | source)
XLA Modules:
  0.0 66.3 jit_solution(2395262169546926977)
XLA Ops:
  0.6 61.6 %shard_map.104 = (f32[5120,128]{1,0:T(8,128)}, f32[32,128]{1,0:T(8,128)}) custom-call(f32[96,256]{1,0:T(8,128)} %bitcast.9, s32[3,512]{1,0:T(4,128)} %stencil_hbm.1, f32[3,512]{1,0:T(4,128)} %weight_hbm.1, s32[1,512]{1,0:T(1,128)} %bitcast.10, s32[1,512]{1,0:T(1,128)} %bitcast.11, bf16[5,3,32,128]{3,2,1,0:T(8,128)(2,1)} %lift_hbm.1, ...), custom_call_target="tpu_custom_call" | custom-call | tf_op jit(solution)/shard_map/pallas_call | solution.py:547
  62.2 0.0 copy-start
  62.2 3.5 %copy.13 = f32[32,5,32,128]{3,2,1,0:T(8,128)} copy(f32[32,5,32,128]{3,2,1,0:T(8,128)} %bitcast.7) | data formatting | bytes 5242880
  65.7 0.0 copy-done
  65.7 0.6 copy.14
Async XLA Ops:
  62.2 3.5 %copy-start = (f32[32,128]{1,0:T(8,128)S(1)}, f32[32,128]{1,0:T(8,128)}, u32[]{:S(2)}) copy-start(f32[32,128]{1,0:T(8,128)} %get-tuple-element.9) | copy-start | bytes 49156

commit v3 on v2

--- a/solution.py
+++ b/solution.py
@@ -352,7 +352,10 @@
             sweep(stages[step - 1], stages[step], x, None)
             return carry
 
-        lax.fori_loop(RIM + step, RIM + rows - step, plane, 0, unroll=2)
+        count = rows - 2 * step
+        lax.fori_loop(
+            RIM + step, RIM + rows - step, plane, 0, unroll=4 if count % 4 == 0 else 2
+        )
 
     def outer(step):
         def plane(i, carry):
@@ -362,7 +365,7 @@
                 sweep(stages[step - 1], stages[step], x, inside)
             return carry
 
-        lax.fori_loop(0, RIM, plane, 0)
+        lax.fori_loop(0, RIM, plane, 0, unroll=5)
 
     for copy in middle:
         copy.wait_recv()

time: 66.5 us -> 64.1 us (0.964)
  Pallas kernels: 61.6 us -> 59.2 us
    pallas_call x1, Pallas kernels: 61.6 us -> 59.2 us  [fast_body(): pl.pallas_call(functools.partial(whole_kernel, slabs, rows, modes_dim, co...]
where the time goes in v3:
time: 64.1 us; the launch traced here: 64 us
  Pallas kernels  59.2 us (92%)
  local copies, waits for them, and re-layouts  4.1 us (6%)
  between operations  0.65 us (1%)
    pallas_call x1, Pallas kernels, fast_body(): pl.pallas_call(functools.partial(whole_kernel, slabs, rows, modes_dim, co...  59.2 us
    unnamed x4, local copies, waits for them, and re-layouts  4.1 us

profile of v3, /device:TPU:0, one launch (start us, length us, event | category | flops | bytes accessed | tf_op | source)
XLA Modules:
  0.0 64.0 jit_solution(17580112058691757975)
XLA Ops:
  0.6 59.2 %shard_map.104 = (f32[5120,128]{1,0:T(8,128)}, f32[32,128]{1,0:T(8,128)}) custom-call(f32[96,256]{1,0:T(8,128)} %bitcast.9, s32[3,512]{1,0:T(4,128)} %stencil_hbm.1, f32[3,512]{1,0:T(4,128)} %weight_hbm.1, s32[1,512]{1,0:T(1,128)} %bitcast.10, s32[1,512]{1,0:T(1,128)} %bitcast.11, bf16[5,3,32,128]{3,2,1,0:T(8,128)(2,1)} %lift_hbm.1, ...), custom_call_target="tpu_custom_call" | custom-call | tf_op jit(solution)/shard_map/pallas_call | solution.py:550
  59.8 0.0 copy-start
  59.9 3.5 %copy.13 = f32[32,5,32,128]{3,2,1,0:T(8,128)} copy(f32[32,5,32,128]{3,2,1,0:T(8,128)} %bitcast.7) | data formatting | bytes 5242880
  63.3 0.0 copy-done
  63.3 0.6 copy.14
Async XLA Ops:
  59.8 3.5 %copy-start = (f32[32,128]{1,0:T(8,128)S(1)}, f32[32,128]{1,0:T(8,128)}, u32[]{:S(2)}) copy-start(f32[32,128]{1,0:T(8,128)} %get-tuple-element.9) | copy-start | bytes 49156
